TPU v7x, 32 devices: a whole 2x2x4 slice. The times are simulated.
32 devices in a mesh: grp: 2 (over y), gx: 4 (over z), gy: 4 (over x, core).
Axes of the slice: x: 2, y: 2, z: 4, core: 2. Of those that a mesh axis runs over, the one named last changes fastest.
Arguments:
- tokens: bfloat16 [1024, 8192], P(('grp', 'gy'), 'gx'), parts along dimension 0, may hold values from -6 to 6
- gate_weight: bfloat16 [8192, 26624], P(None, ('gy', 'gx')), may hold values from -0.0625 to 0.0625
- up_weight: bfloat16 [8192, 26624], P(None, ('gy', 'gx')), may hold values from -0.0625 to 0.0625
- down_weight: bfloat16 [26624, 8192], P('gy', 'gx'), may hold values from -0.0390625 to 0.0390625
Outputs:
- mixed: bfloat16 [1024, 8192], P(('grp', 'gy'), 'gx'), parts along dimension 0
There are 2 independent parts, one for each index of `grp`. A program takes and returns all parts, laid end to end along the dimension named above; an argument that names none is the same for every part. Nothing has to cross between parts.
All inputs are finite; a program needn't handle non-finite values.
Results may differ from a plain program's by a relative error of at most 0.0051.
Values may be sent and summed in bfloat16 or wider, within the bound.
A program may use at most 192 MiB of HBM per device.

v0:
```python
import jax
import jax.numpy as jnp
from jax import lax
from jax.sharding import PartitionSpec as P


def shards(tokens, gate_weight, up_weight, down_weight):
    all_rows = lax.all_gather(tokens, "gy", axis=0, tiled=True)
    shard_piece = lax.all_gather(all_rows, "gx", axis=1, tiled=True)
    gate_next = jnp.dot(shard_piece, gate_weight, preferred_element_type=jnp.float32)
    up_next = jnp.dot(shard_piece, up_weight, preferred_element_type=jnp.float32)
    hidden = (jax.nn.silu(gate_next) * up_next).astype(jnp.bfloat16)
    partial_value = jnp.dot(
        lax.all_gather(hidden, "gx", axis=1, tiled=True),
        down_weight,
        preferred_element_type=jnp.float32,
    )
    return lax.psum_scatter(partial_value, "gy", scatter_dimension=0, tiled=True).astype(
        jnp.bfloat16
    )


def solution(mesh):
    placed = (P(("grp", "gy"), "gx"), P(None, ("gy", "gx")), P(None, ("gy", "gx")), P("gy", "gx"))
    return jax.shard_map(
        shards, mesh=mesh, in_specs=placed, out_specs=P(("grp", "gy"), "gx"), check_vma=False
    )
```

profile of v0, /device:TPU:0, one launch (start us, length us, event | category | flops | bytes accessed | tf_op | source)
XLA Modules:
  0.0 423.9 jit_solution(13815366351405985682)
XLA Ops:
  6.5 0.0 all-gather.4.cloned.1.call-start
  6.5 0.7 all-gather.4.cloned.1.call-update
  7.3 0.0 all-gather.6.cloned.1.call-start
  7.3 26.9 %all-gather.4.cloned.1.call-done = bf16[512,2048]{1,0:T(8,128)(2,1)} async-done(((bf16[128,2048]{1,0:T(8,128)(2,1)}), bf16[512,2048]{1,0:T(8,128)(2,1)}) %all-gather.4.cloned.1.call-update) | async-done | bytes 2097168 | tf_op jit(solution)/shard_map/all_gather | solution.py:8
  34.2 0.0 all-gather.6.cloned.1.call-update
  34.3 0.0 all-gather.8.cloned.1.call-start
  34.3 151.2 %all-gather.6.cloned.1.call-done = bf16[512,8192]{1,0:T(8,128)(2,1)} async-done(((bf16[512,2048]{1,0:T(8,128)(2,1)}), bf16[512,8192]{1,0:T(8,128)(2,1)}) %all-gather.6.cloned.1.call-update) | async-done | bytes 8388624 | tf_op jit(solution)/shard_map/all_gather | solution.py:9
  185.5 0.0 copy-start
  185.5 21.0 %fusion = f32[512,1664]{1,0:T(8,128)S(1)} fusion(bf16[512,8192]{1,0:T(8,128)(2,1)} %all-gather.6.cloned.1.call-done, bf16[8192,1664]{1,0:T(8,128)(2,1)} %param.5), kind=kOutput, calls=%fused_computation.1 | convolution fusion | flops 13958643712 | bytes 39059456 | tf_op jit(solution)/shard_map/dot_general | solution.py:10
  206.5 0.0 copy-done
  206.5 21.1 %multiply_convert_fusion = bf16[512,1664]{1,0:T(8,128)(2,1)} fusion(f32[512,1664]{1,0:T(8,128)S(1)} %fusion, bf16[512,8192]{1,0:T(8,128)(2,1)S(1)} %copy-done, bf16[8192,1664]{1,0:T(8,128)(2,1)} %param.6), kind=kOutput, calls=%fused_computation | convolution fusion | flops 13963755520 | bytes 40763392 | tf_op jit(solution)/shard_map/dot_general | solution.py:11
  227.6 0.0 all-gather.8.cloned.1.call-update
  227.6 0.2 reduce-scatter.2.cloned.1.call-start
  227.8 122.0 %all-gather.8.cloned.1.call-done = bf16[512,6656]{1,0:T(8,128)(2,1)} async-done(((bf16[512,1664]{1,0:T(8,128)(2,1)}), bf16[512,6656]{1,0:T(8,128)(2,1)}) %all-gather.8.cloned.1.call-update) | async-done | bytes 6815760 | tf_op jit(solution)/shard_map/all_gather | solution.py:14
  349.8 22.6 %fusion.1 = f32[512,2048]{1,0:T(8,128)} fusion(bf16[512,6656]{1,0:T(8,128)(2,1)} %all-gather.8.cloned.1.call-done, bf16[6656,2048]{1,0:T(8,128)(2,1)} %param.7), kind=kOutput, calls=%fused_computation.2 | convolution fusion | flops 13958643712 | bytes 38273024 | tf_op jit(solution)/shard_map/dot_general | solution.py:13
  372.4 0.0 reduce-scatter.2.cloned.1.call-update
  372.5 42.8 %reduce-scatter.2.cloned.1.call-done = f32[128,2048]{1,0:T(8,128)} async-done(((f32[512,2048]{1,0:T(8,128)}), f32[128,2048]{1,0:T(8,128)}) %reduce-scatter.2.cloned.1.call-update) | async-done | bytes 1048592 | tf_op jit(solution)/shard_map/reduce_scatter | solution.py:18
  415.3 2.1 convert_element_type.7
Async XLA Ops:
  6.5 27.7 %all-gather.4.cloned.1.call-start = ((), (), s32[]{:S(2)}) async-start(), calls=%async_computation.1 | async-start | bytes 2621440 | tf_op jit(solution)/shard_map/all_gather | solution.py:8
  7.3 178.2 %all-gather.6.cloned.1.call-start = ((), (), s32[]{:S(2)}) async-start(), calls=%async_computation.2 | async-start | bytes 10485760 | tf_op jit(solution)/shard_map/all_gather | solution.py:9
  34.3 315.6 %all-gather.8.cloned.1.call-start = ((), (), s32[]{:S(2)}) async-start(), calls=%async_computation.3 | async-start | bytes 8519680 | tf_op jit(solution)/shard_map/all_gather | solution.py:14
  185.5 21.0 %copy-start = (bf16[512,8192]{1,0:T(8,128)(2,1)S(1)}, bf16[512,8192]{1,0:T(8,128)(2,1)}, u32[]{:S(2)}) copy-start(bf16[512,8192]{1,0:T(8,128)(2,1)} %all-gather.6.cloned.1.call-done) | copy-start | bytes 25165828
  227.6 187.7 %reduce-scatter.2.cloned.1.call-start = ((), (), s32[]{:S(2)}) async-start(), calls=%async_computation.4 | async-start | bytes 5242880 | tf_op jit(solution)/shard_map/reduce_scatter | solution.py:18
Sparse Core Ops, SparseCore 0:
  8.9 25.2 all-gather.3
  35.8 149.6 all-gather.5
  227.7 122.0 all-gather.7
  372.6 42.6 reduce-scatter.1
where the time goes:
time: 424 us
  waiting for transfers between devices  344 us (81%)
  matrix products  64.7 us (15%)
  between operations  13.1 us (3%)
    all_gather x1, waiting for transfers between devices, shards(): shard_piece = lax.all_gather(all_rows, 'gx', axis=1, tiled=True)  151 us
    all_gather x1, waiting for transfers between devices, shards(): lax.all_gather(hidden, 'gx', axis=1, tiled=True)  122 us
    reduce_scatter x1, waiting for transfers between devices, shards(): lax.psum_scatter(partial_value, 'gy', scatter_dimension=0, tiled=True)  42.8 us
    all_gather x1, waiting for transfers between devices, shards(): all_rows = lax.all_gather(tokens, 'gy', axis=0, tiled=True)  26.9 us
    dot_general x1, matrix products, shards(): jnp.dot(lax.all_gather(hidden, 'gx', axis=1, tiled=True), down_weight, pr...  22.6 us
    dot_general x1, matrix products, shards(): jnp.dot(shard_piece, up_weight, preferred_element_type=jnp.float32)  21.1 us
    dot_general x1, matrix products, shards(): jnp.dot(shard_piece, gate_weight, preferred_element_type=jnp.float32)  21 us
  transfers between devices with their start and end apart: 4, of which 4 were waited for; matrix products, arithmetic and copies ran while one was open for 0% of the time, Pallas kernels for 0%

commit v1 on v0

v1 whole, which is shorter than its diff:
```python
import jax
import jax.numpy as jnp
from jax import lax
from jax.sharding import PartitionSpec as P

CHUNKS = 2


def shards(tokens, gate_weight, up_weight, down_weight):
    rows = tokens.shape[0] // CHUNKS
    pieces = []
    for at in range(CHUNKS):
        own = tokens[at * rows : (at + 1) * rows]
        wide = lax.all_gather(own, "gx", axis=1, tiled=True)
        pieces.append(lax.all_gather(wide, "gy", axis=0, tiled=True))
    outs = []
    for piece in pieces:
        gate_next = jnp.dot(piece, gate_weight, preferred_element_type=jnp.float32)
        up_next = jnp.dot(piece, up_weight, preferred_element_type=jnp.float32)
        hidden = (jax.nn.silu(gate_next) * up_next).astype(jnp.bfloat16)
        partial_value = jnp.dot(
            lax.all_gather(hidden, "gx", axis=1, tiled=True),
            down_weight,
            preferred_element_type=jnp.float32,
        )
        outs.append(
            lax.psum_scatter(partial_value, "gy", scatter_dimension=0, tiled=True).astype(jnp.bfloat16)
        )
    return jnp.concatenate(outs, axis=0)


def solution(mesh):
    placed = (P(("grp", "gy"), "gx"), P(None, ("gy", "gx")), P(None, ("gy", "gx")), P("gy", "gx"))
    return jax.shard_map(
        shards, mesh=mesh, in_specs=placed, out_specs=P(("grp", "gy"), "gx"), check_vma=False
    )
```

time: 424 us -> 353 us (0.83)
  waiting for transfers between devices: 344 us -> 236 us
  matrix products: 64.7 us -> 97.3 us
    all_gather x2 -> x4, waiting for transfers between devices: 178 us -> 97.2 us  [the longest x2 59.3 us: shards(): wide = lax.all_gather(own, 'gx', axis=1, tiled=True)]
    all_gather x1 -> x2, waiting for transfers between devices: 122 us -> 88.4 us  [shards(): lax.all_gather(hidden, 'gx', axis=1, tiled=True)]
    dot_general x2 -> x4, matrix products: 42.1 us -> 66.4 us  [the longest x2 38 us: shards(): gate_next = jnp.dot(piece, gate_weight, preferred_element_type=jnp.float32)]
    dot_general x1 -> x2, matrix products: 22.6 us -> 30.9 us  [shards(): jnp.dot(lax.all_gather(hidden, 'gx', axis=1, tiled=True), down_weight, pr...]
    reduce_scatter x1 -> x2, waiting for transfers between devices: 42.8 us -> 50.1 us  [shards(): lax.psum_scatter(partial_value, 'gy', scatter_dimension=0, tiled=True)]
  transfers between devices with their start and end apart: 4 -> 8, of which waited for: 4 -> 8; matrix products, arithmetic and copies ran while one was open for 0% -> 28% of each run, Pallas kernels for 0% -> 0%
where the time goes in v1:
time: 353 us
  waiting for transfers between devices  236 us (67%)
  matrix products  97.3 us (28%)
  between operations  13.5 us (4%)
    all_gather x2, waiting for transfers between devices, shards(): lax.all_gather(hidden, 'gx', axis=1, tiled=True)  88.4 us
    all_gather x2, waiting for transfers between devices, shards(): wide = lax.all_gather(own, 'gx', axis=1, tiled=True)  59.3 us
    reduce_scatter x2, waiting for transfers between devices, shards(): lax.psum_scatter(partial_value, 'gy', scatter_dimension=0, tiled=True)  50.1 us
    dot_general x2, matrix products, shards(): gate_next = jnp.dot(piece, gate_weight, preferred_element_type=jnp.float32)  38 us
    all_gather x2, waiting for transfers between devices, shards(): pieces.append(lax.all_gather(wide, 'gy', axis=0, tiled=True))  37.8 us
    dot_general x2, matrix products, shards(): jnp.dot(lax.all_gather(hidden, 'gx', axis=1, tiled=True), down_weight, pr...  30.9 us
    dot_general x2, matrix products, shards(): up_next = jnp.dot(piece, up_weight, preferred_element_type=jnp.float32)  28.5 us
  transfers between devices with their start and end apart: 8, of which 8 were waited for; matrix products, arithmetic and copies ran while one was open for 28% of the time, Pallas kernels for 0%

profile of v1, /device:TPU:0, one launch (start us, length us, event | category | flops | bytes accessed | tf_op | source)
XLA Modules:
  0.0 352.9 jit_solution(16686140465058904127)
XLA Ops:
  6.5 0.0 all-gather.7.cloned.1.call-start
  6.5 1.9 fusion.2
  8.4 0.0 all-gather.7.cloned.1.call-update
  8.4 0.0 all-gather.13.cloned.1.call-start
  8.5 0.7 all-gather.13.cloned.1.call-update
  9.2 0.0 all-gather.9.cloned.1.call-start
  9.2 30.4 %all-gather.7.cloned.1.call-done = bf16[64,8192]{1,0:T(8,128)(2,1)} async-done(((bf16[64,2048]{1,0:T(8,128)(2,1)}), bf16[64,8192]{1,0:T(8,128)(2,1)}) %all-gather.7.cloned.1.call-update) | async-done | bytes 1048592 | tf_op jit(solution)/shard_map/all_gather | solution.py:14
  39.6 0.0 all-gather.9.cloned.1.call-update
  39.6 0.0 all-gather.15.cloned.1.call-start
  39.7 29.0 %all-gather.13.cloned.1.call-done = bf16[64,8192]{1,0:T(8,128)(2,1)} async-done(((bf16[64,2048]{1,0:T(8,128)(2,1)}), bf16[64,8192]{1,0:T(8,128)(2,1)}) %all-gather.13.cloned.1.call-update) | async-done | bytes 1048592 | tf_op jit(solution)/shard_map/all_gather | solution.py:14
  68.6 0.0 all-gather.15.cloned.1.call-update
  68.6 0.0 all-gather.11.cloned.1.call-start
  68.7 35.5 %all-gather.9.cloned.1.call-done = bf16[256,8192]{1,0:T(8,128)(2,1)} async-done(((bf16[64,8192]{1,0:T(8,128)(2,1)}), bf16[256,8192]{1,0:T(8,128)(2,1)}) %all-gather.9.cloned.1.call-update) | async-done | bytes 4194320 | tf_op jit(solution)/shard_map/all_gather | solution.py:15
  104.2 0.0 copy-start.1
  104.2 19.1 %fusion.3 = f32[256,1664]{1,0:T(8,128)S(1)} fusion(bf16[256,8192]{1,0:T(8,128)(2,1)} %all-gather.9.cloned.1.call-done, bf16[8192,1664]{1,0:T(8,128)(2,1)} %param.5), kind=kOutput, calls=%fused_computation.6 | convolution fusion | flops 6979321856 | bytes 33161216 | tf_op jit(solution)/shard_map/dot_general | solution.py:18
  123.3 0.0 copy-done.1
  123.3 14.2 %fusion = bf16[256,1664]{1,0:T(8,128)(2,1)} fusion(bf16[256,8192]{1,0:T(8,128)(2,1)S(1)} %copy-done.1, bf16[8192,1664]{1,0:T(8,128)(2,1)} %param.6, f32[256,1664]{1,0:T(8,128)S(1)} %fusion.3), kind=kOutput, calls=%fused_computation.2 | convolution fusion | flops 6981877760 | bytes 34013184 | tf_op jit(solution)/shard_map/dot_general | solution.py:19
  137.5 0.0 all-gather.11.cloned.1.call-update
  137.6 0.2 all-gather.17.cloned.1.call-start
  137.8 2.3 all-gather.15.cloned.1.call-done
  140.1 0.0 copy-start
  140.1 18.9 %fusion.5 = f32[256,1664]{1,0:T(8,128)S(1)} fusion(bf16[256,8192]{1,0:T(8,128)(2,1)} %all-gather.15.cloned.1.call-done, bf16[8192,1664]{1,0:T(8,128)(2,1)} %param.5), kind=kOutput, calls=%fused_computation.8 | convolution fusion | flops 6979321856 | bytes 33161216 | tf_op jit(solution)/shard_map/dot_general | solution.py:18
  159.0 0.0 copy-done
  159.0 14.2 %fusion.1 = bf16[256,1664]{1,0:T(8,128)(2,1)} fusion(bf16[256,8192]{1,0:T(8,128)(2,1)S(1)} %copy-done, bf16[8192,1664]{1,0:T(8,128)(2,1)} %param.6, f32[256,1664]{1,0:T(8,128)S(1)} %fusion.5), kind=kOutput, calls=%fused_computation.3 | convolution fusion | flops 6981877760 | bytes 34013184 | tf_op jit(solution)/shard_map/dot_general | solution.py:19
  173.3 0.0 all-gather.17.cloned.1.call-update
  173.3 0.0 reduce-scatter.3.cloned.1.call-start
  173.3 36.0 %all-gather.11.cloned.1.call-done = bf16[256,6656]{1,0:T(8,128)(2,1)} async-done(((bf16[256,1664]{1,0:T(8,128)(2,1)}), bf16[256,6656]{1,0:T(8,128)(2,1)}) %all-gather.11.cloned.1.call-update) | async-done | bytes 3407888 | tf_op jit(solution)/shard_map/all_gather | solution.py:22
  209.4 15.3 %fusion.4 = f32[256,2048]{1,0:T(8,128)} fusion(bf16[256,6656]{1,0:T(8,128)(2,1)} %all-gather.11.cloned.1.call-done, bf16[6656,2048]{1,0:T(8,128)(2,1)} %param.7), kind=kOutput, calls=%fused_computation.7 | convolution fusion | flops 6979321856 | bytes 32768000 | tf_op jit(solution)/shard_map/dot_general | solution.py:21
  224.7 0.0 reduce-scatter.3.cloned.1.call-update
  224.7 0.3 reduce-scatter.5.cloned.1.call-start
  225.0 52.3 %all-gather.17.cloned.1.call-done = bf16[256,6656]{1,0:T(8,128)(2,1)} async-done(((bf16[256,1664]{1,0:T(8,128)(2,1)}), bf16[256,6656]{1,0:T(8,128)(2,1)}) %all-gather.17.cloned.1.call-update) | async-done | bytes 3407888 | tf_op jit(solution)/shard_map/all_gather | solution.py:22
  277.3 15.6 %fusion.6 = f32[256,2048]{1,0:T(8,128)} fusion(bf16[256,6656]{1,0:T(8,128)(2,1)} %all-gather.17.cloned.1.call-done, bf16[6656,2048]{1,0:T(8,128)(2,1)} %param.7), kind=kOutput, calls=%fused_computation.9 | convolution fusion | flops 6979321856 | bytes 32768000 | tf_op jit(solution)/shard_map/dot_general | solution.py:21
  292.9 0.0 reduce-scatter.5.cloned.1.call-update
  292.9 17.0 %reduce-scatter.3.cloned.1.call-done = f32[64,2048]{1,0:T(8,128)} async-done(((f32[256,2048]{1,0:T(8,128)}), f32[64,2048]{1,0:T(8,128)}) %reduce-scatter.3.cloned.1.call-update) | async-done | bytes 524304 | tf_op jit(solution)/shard_map/reduce_scatter | solution.py:27
  309.9 1.1 convert_element_type.13
  311.0 33.1 %reduce-scatter.5.cloned.1.call-done = f32[64,2048]{1,0:T(8,128)} async-done(((f32[256,2048]{1,0:T(8,128)}), f32[64,2048]{1,0:T(8,128)}) %reduce-scatter.5.cloned.1.call-update) | async-done | bytes 524304 | tf_op jit(solution)/shard_map/reduce_scatter | solution.py:27
  344.1 1.1 convert_element_type.15
  345.2 0.8 pad_maximum_fusion
Async XLA Ops:
  6.5 33.1 %all-gather.7.cloned.1.call-start = ((), (), s32[]{:S(2)}) async-start(), calls=%async_computation.2 | async-start | bytes 1310720 | tf_op jit(solution)/shard_map/all_gather | solution.py:14
  8.4 60.2 %all-gather.13.cloned.1.call-start = ((), (), s32[]{:S(2)}) async-start(), calls=%async_computation.6 | async-start | bytes 1310720 | tf_op jit(solution)/shard_map/all_gather | solution.py:14
  9.2 95.0 %all-gather.9.cloned.1.call-start = ((), (), s32[]{:S(2)}) async-start(), calls=%async_computation.3 | async-start | bytes 5242880 | tf_op jit(solution)/shard_map/all_gather | solution.py:15
  39.6 100.5 %all-gather.15.cloned.1.call-start = ((), (), s32[]{:S(2)}) async-start(), calls=%async_computation.7 | async-start | bytes 5242880 | tf_op jit(solution)/shard_map/all_gather | solution.py:15
  68.6 140.7 %all-gather.11.cloned.1.call-start = ((), (), s32[]{:S(2)}) async-start(), calls=%async_computation.4 | async-start | bytes 4259840 | tf_op jit(solution)/shard_map/all_gather | solution.py:22
  104.2 19.1 %copy-start.1 = (bf16[256,8192]{1,0:T(8,128)(2,1)S(1)}, bf16[256,8192]{1,0:T(8,128)(2,1)}, u32[]{:S(2)}) copy-start(bf16[256,8192]{1,0:T(8,128)(2,1)} %all-gather.9.cloned.1.call-done) | copy-start | bytes 12582916
  137.6 139.8 %all-gather.17.cloned.1.call-start = ((), (), s32[]{:S(2)}) async-start(), calls=%async_computation.8 | async-start | bytes 4259840 | tf_op jit(solution)/shard_map/all_gather | solution.py:22
  140.1 18.9 %copy-start = (bf16[256,8192]{1,0:T(8,128)(2,1)S(1)}, bf16[256,8192]{1,0:T(8,128)(2,1)}, u32[]{:S(2)}) copy-start(bf16[256,8192]{1,0:T(8,128)(2,1)} %all-gather.15.cloned.1.call-done) | copy-start | bytes 12582916
  173.3 136.6 %reduce-scatter.3.cloned.1.call-start = ((), (), s32[]{:S(2)}) async-start(), calls=%async_computation.5 | async-start | bytes 2621440 | tf_op jit(solution)/shard_map/reduce_scatter | solution.py:27
  224.7 119.4 %reduce-scatter.5.cloned.1.call-start = ((), (), s32[]{:S(2)}) async-start(), calls=%async_computation.9 | async-start | bytes 2621440 | tf_op jit(solution)/shard_map/reduce_scatter | solution.py:27
Sparse Core Ops, SparseCore 0:
  8.9 30.6 all-gather.6
  41.2 27.4 all-gather.12
  70.2 33.9 all-gather.8
  105.6 34.4 all-gather.14
  141.6 67.7 all-gather.10
  210.8 66.4 all-gather.16
  279.8 30.0 reduce-scatter.2
  312.6 31.4 reduce-scatter.4

commit v2 on v1

--- a/solution.py
+++ b/solution.py
@@ -1,9 +1,16 @@
+import functools
+
 import jax
 import jax.numpy as jnp
 from jax import lax
+from jax.experimental import pallas as pl
+from jax.experimental.pallas import tpu as pltpu
 from jax.sharding import PartitionSpec as P
 
 CHUNKS = 2
+PARTS = 4
+TILE = 128
+WIDE = 256
 
 
 def shards(tokens, gate_weight, up_weight, down_weight):
@@ -29,8 +36,370 @@
     return jnp.concatenate(outs, axis=0)
 
 
+def kernel(
+    nz, tokens, gate, up, down, out,
+    tok, hid, wts, dn, acc, r1, r2,
+    own_sem, w_sem, dn_sem, tz_s, tz_r, ts_s, ts_r, tx_s, tx_r, tf_s, tf_r, hz_s, hz_r,
+    r1_s, r1_r, r2_s, r2_r,
+):
+    z, g = lax.axis_index("gx"), lax.axis_index("gy")
+    core, x = g % 2, g // 2
+    sib, across = 2 * x + 1 - core, 2 * (1 - x) + core
+    rows = tokens.shape[0] // PARTS
+    units = gate.shape[1]
+    tiles = units // TILE
+    depth = tokens.shape[1]
+    f32 = jnp.float32
+
+    def remote(src, dst, s, r, **to):
+        return pltpu.make_async_remote_copy(
+            src_ref=src, dst_ref=dst, send_sem=s, recv_sem=r, device_id=to,
+            device_id_type=pl.DeviceIdType.MESH,
+        )
+
+    def token_block(c, who, b):
+        place = (who % 2) * 2 + who // 2
+        return tok.at[c, b, pl.ds(pl.multiple_of(place * rows, rows), rows), :]
+
+    def hop(view, send, recv, way, c, s):
+        b = z - (s - 1) if way == 0 else z + (s - 1)
+        to = z + 1 if way == 0 else z - 1
+        live = (b >= 0) & (z < nz - 1) if way == 0 else (b < nz) & (z > 0)
+        ref = lambda: view(c, b)
+        make = lambda: remote(ref(), ref(), send.at[way, c, s - 1], recv.at[way, c, s - 1], gx=to)
+        return live, make
+
+    def hop_start(view, send, recv, c, s):
+        for way in range(2):
+            live, make = hop(view, send, recv, way, c, s)
+
+            @pl.when(live & (s < nz))
+            def _():
+                make().start()
+
+    def hop_sent(view, send, recv, c, s):
+        for way in range(2):
+            live, make = hop(view, send, recv, way, c, s)
+
+            @pl.when(live)
+            def _():
+                make().wait_send()
+
+    def hop_recv(view, send, recv, c, s, then):
+        for way in range(2):
+            b = z - s if way == 0 else z + s
+            back = z - 1 if way == 0 else z + 1
+
+            @pl.when(b >= 0 if way == 0 else b < nz)
+            def _():
+                remote(
+                    view(c, b), view(c, b), send.at[way, c, s - 1], recv.at[way, c, s - 1], gx=back
+                ).wait_recv()
+                live, make = hop(view, send, recv, way, c, s + 1)
+
+                @pl.when(live)
+                def _():
+                    make().start()
+
+                if then is not None:
+                    then(c, b)
+
+    token_view = lambda c, b: token_block(c, g, b)
+    hidden_view = lambda c, b: hid.at[c, b]
+    tokens_z = (token_view, tz_s, tz_r)
+    hidden_z = (hidden_view, hz_s, hz_r)
+
+    def to_sib(c, b, who, s, r):
+        return remote(token_block(c, who, b), token_block(c, who, b), s.at[c, b], r.at[c, b], gy=sib)
+
+    def to_across(c, b, who):
+        return remote(
+            token_block(c, who, b), token_block(c, who, b), tx_s.at[c, b], tx_r.at[c, b], gy=across
+        )
+
+    def spread(c, b):
+        to_across(c, b, g).start()
+        to_sib(c, b, g, ts_s, ts_r).start()
+
+    def tokens_out(c):
+        hop_start(*tokens_z, c, 1)
+        spread(c, z)
+
+    def tokens_step(c, s):
+        hop_recv(*tokens_z, c, s, spread)
+
+    def tokens_across(c):
+        @pl.loop(0, nz)
+        def _(b):
+            to_across(c, b, across).wait_recv()
+            to_sib(c, b, across, tf_s, tf_r).start()
+
+    def tokens_ready(c):
+        @pl.loop(0, nz)
+        def _(b):
+            to_sib(c, b, sib, ts_s, ts_r).wait_recv()
+            to_sib(c, b, 2 * (1 - x) + 1 - core, tf_s, tf_r).wait_recv()
+
+    def weight_copies(i):
+        t, slot = i % tiles, i % 2
+        cols = pl.ds(pl.multiple_of(t * TILE, TILE), TILE)
+        return [
+            pltpu.make_async_copy(
+                ref.at[:, cols], wts.at[slot, :, pl.ds(at * TILE, TILE)], w_sem.at[slot, at]
+            )
+            for at, ref in enumerate((gate, up))
+        ]
+
+    def own_copy(c):
+        return pltpu.make_async_copy(
+            tokens.at[pl.ds(pl.multiple_of(c * rows, rows), rows), :], token_block(c, g, z), own_sem.at[c]
+        )
+
+    for c in range(PARTS):
+        own_copy(c).start()
+    for copy in weight_copies(0):
+        copy.start()
+    load_down = pltpu.make_async_copy(down, dn, dn_sem)
+    load_down.start()
+
+    barrier = pltpu.get_barrier_semaphore()
+    for who in (sib, across):
+        pl.semaphore_signal(
+            barrier, inc=1, device_id={"gy": who}, device_id_type=pl.DeviceIdType.MESH
+        )
+
+    @pl.when(z > 0)
+    def _():
+        pl.semaphore_signal(
+            barrier, inc=1, device_id={"gx": z - 1}, device_id_type=pl.DeviceIdType.MESH
+        )
+
+    @pl.when(z < nz - 1)
+    def _():
+        pl.semaphore_signal(
+            barrier, inc=1, device_id={"gx": z + 1}, device_id_type=pl.DeviceIdType.MESH
+        )
+
+    pl.semaphore_wait(barrier, 2 + jnp.where(z > 0, 1, 0) + jnp.where(z < nz - 1, 1, 0))
+
+    for c in range(PARTS):
+        own_copy(c).wait()
+    tokens_out(0)
+    tokens_out(1)
+
+    @pl.loop(1, nz)
+    def _(s):
+        tokens_step(0, s)
+
+    tokens_across(0)
+
+    last = nz - 1
+    early = 2 * (PARTS - 1) - 1
+
+    def hidden_step(n):
+        hop_recv(*hidden_z, n // last, n % last + 1, None)
+
+    @pl.loop(0, PARTS)
+    def _(c):
+        tokens_ready(c)
+
+        @pl.loop(0, tiles)
+        def _(t):
+            i = c * tiles + t
+
+            @pl.when(i + 1 < PARTS * tiles)
+            def _():
+                for copy in weight_copies(i + 1):
+                    copy.start()
+
+            for copy in weight_copies(i):
+                copy.wait()
+            slot = i % 2
+            total = None
+            for b in range(nz):
+                part = jnp.dot(
+                    tok[c, b], wts[slot, pl.ds(b * depth, depth), :], preferred_element_type=f32
+                )
+                total = part if total is None else total + part
+            a, u = total[:, :TILE], total[:, TILE:]
+            hid[c, z, :, pl.ds(pl.multiple_of(t * TILE, TILE), TILE)] = (
+                a / (1.0 + jnp.exp(-a)) * u
+            ).astype(hid.dtype)
+
+            @pl.when((c == 0) & (t < nz * (PARTS - 1)))
+            def _():
+                which, s = 1 + t // nz, t % nz + 1
+
+                @pl.when((s == 1) & (which + 1 < PARTS))
+                def _():
+                    tokens_out(which + 1)
+
+                @pl.when(s < nz)
+                def _():
+                    tokens_step(which, s)
+
+                @pl.when(s == nz)
+                def _():
+                    tokens_across(which)
+
+            @pl.when((c >= 2) & (t == tiles // 2))
+            def _():
+                hidden_step(2 * (c - 1) - 1)
+
+        hop_start(*hidden_z, c, 1)
+
+        @pl.when(c >= 1)
+        def _():
+            hidden_step(2 * (c - 1))
+
+    load_down.wait()
+
+    def mix(d, b, first):
+        @pl.loop(0, acc.shape[2] // WIDE)
+        def _(n):
+            cols = pl.ds(pl.multiple_of(n * WIDE, WIDE), WIDE)
+            value = jnp.dot(
+                hid[d, b],
+                dn[pl.ds(pl.multiple_of(b * units, TILE), units), cols],
+                preferred_element_type=f32,
+            )
+            acc[d, :, cols] = value if first else acc[d, :, cols] + value
+
+    half = 2 * rows
+    core_rows = lambda who: pl.ds(pl.multiple_of(who * half, half), half)
+    place_rows = lambda at: pl.ds(pl.multiple_of((core * 2 + at) * rows, rows), rows)
+
+    def sum_sib(d):
+        return remote(acc.at[d, core_rows(1 - core)], r1.at[d], r1_s.at[d], r1_r.at[d], gy=sib)
+
+    def sum_across(d):
+        return remote(acc.at[d, place_rows(1 - x)], r2.at[d], r2_s.at[d], r2_r.at[d], gy=across)
+
+    def second(d):
+        sum_sib(d).wait_recv()
+        acc[d, core_rows(core), :] += r1[d]
+        sum_across(d).start()
+
+    def third(d):
+        sum_across(d).wait_recv()
+        out[pl.ds(pl.multiple_of(d * rows, rows), rows), :] = (
+            acc[d, place_rows(x), :] + r2[d]
+        ).astype(out.dtype)
+
+    @pl.loop(0, PARTS)
+    def _(d):
+        mix(d, z, True)
+
+        @pl.loop(1, nz)
+        def _(s):
+            n = d * last + s - 1
+
+            @pl.when(n >= early)
+            def _():
+                hidden_step(n)
+
+            @pl.when(z - s >= 0)
+            def _():
+                mix(d, z - s, False)
+
+            @pl.when(z + s < nz)
+            def _():
+                mix(d, z + s, False)
+
+        sum_sib(d).start()
+
+        @pl.when(d >= 1)
+        def _():
+            second(d - 1)
+
+        @pl.when(d >= 2)
+        def _():
+            third(d - 2)
+
+    second(PARTS - 1)
+    third(PARTS - 2)
+    third(PARTS - 1)
+
+    @pl.loop(0, PARTS)
+    def _(c):
+        @pl.loop(1, nz)
+        def _(s):
+            hop_sent(*tokens_z, c, s)
+            hop_sent(*hidden_z, c, s)
+
+        @pl.loop(0, nz)
+        def _(b):
+            to_across(c, b, g).wait_send()
+            to_sib(c, b, g, ts_s, ts_r).wait_send()
+            to_sib(c, b, across, tf_s, tf_r).wait_send()
+
+        sum_sib(c).wait_send()
+        sum_across(c).wait_send()
+
+
+def fused(nz, tokens, gate_weight, up_weight, down_weight):
+    own, depth = tokens.shape
+    units, cols = gate_weight.shape[1], down_weight.shape[1]
+    rows = own // PARTS
+    whole = 4 * rows
+    dma = pltpu.SemaphoreType.DMA
+    bf16 = jnp.bfloat16
+    anywhere = pl.BlockSpec(memory_space=pl.ANY)
+    hops, each = dma((2, PARTS, nz - 1)), dma((PARTS, nz))
+    one = dma((PARTS,))
+    return pl.pallas_call(
+        functools.partial(kernel, nz),
+        out_shape=jax.ShapeDtypeStruct((own, cols), bf16),
+        in_specs=[anywhere] * 4,
+        out_specs=pl.BlockSpec(memory_space=pltpu.VMEM),
+        scratch_shapes=[
+            pltpu.VMEM((PARTS, nz, whole, depth), bf16),
+            pltpu.VMEM((PARTS, nz, whole, units), bf16),
+            pltpu.VMEM((2, nz * depth, 2 * TILE), bf16),
+            pltpu.VMEM(down_weight.shape, bf16),
+            pltpu.VMEM((PARTS, whole, cols), jnp.float32),
+            pltpu.VMEM((PARTS, 2 * rows, cols), jnp.float32),
+            pltpu.VMEM((PARTS, rows, cols), jnp.float32),
+            one, dma((2, 2)), dma(()),
+            hops, hops, each, each, each, each, each, each, hops, hops,
+            one, one, one, one,
+        ],
+        compiler_params=pltpu.CompilerParams(
+            collective_id=0, has_side_effects=True, vmem_limit_bytes=62 * 2**20
+        ),
+        cost_estimate=pl.CostEstimate(
+            flops=2 * 4 * own * (2 * nz * depth * units + nz * units * cols),
+            bytes_accessed=2 * (2 * PARTS * nz * depth * units + nz * units * cols),
+            transcendentals=4 * own * units,
+        ),
+    )(tokens, gate_weight, up_weight, down_weight)
+
+
+def fits(mesh):
+    def body(nz, tokens, gate_weight, up_weight, down_weight):
+        own, depth = tokens.shape
+        units, cols = gate_weight.shape[1], down_weight.shape[1]
+        held = (
+            2 * 4 * own * nz * (depth + units) + 8 * nz * depth * TILE
+            + 2 * nz * units * cols + 4 * own * cols * 7 + 2 * own * cols
+        )
+        tiles = units // TILE
+        return (
+            mesh.shape["gy"] == 4 and nz > 1 and own % (16 * PARTS) == 0 and units % TILE == 0
+            and depth % TILE == 0 and cols % WIDE == 0 and held <= 61 * 2**20
+            and tiles >= nz * (PARTS - 1) and (PARTS - 1) * 2 - 1 <= PARTS * (nz - 1)
+        )
+    return body
+
+
 def solution(mesh):
     placed = (P(("grp", "gy"), "gx"), P(None, ("gy", "gx")), P(None, ("gy", "gx")), P("gy", "gx"))
+    nz = mesh.shape["gx"]
+    ok = fits(mesh)
+
+    def body(*args):
+        return fused(nz, *args) if ok(nz, *args) else shards(*args)
+
     return jax.shard_map(
-        shards, mesh=mesh, in_specs=placed, out_specs=P(("grp", "gy"), "gx"), check_vma=False
+        body, mesh=mesh, in_specs=placed, out_specs=P(("grp", "gy"), "gx"), check_vma=False
     )

time: 353 us -> 210 us (0.59)
  waiting for transfers between devices: 236 us -> 0 us
  Pallas kernels: 0 us -> 208 us
  matrix products: 97.3 us -> 0 us
  between operations: 13.5 us -> 0.01 us
    pallas_call x0 -> x1, Pallas kernels: none -> 208 us  [fused(): pl.pallas_call(functools.partial(kernel, nz), out_shape=jax.ShapeDtypeStr...]
    all_gather x6 -> x0, waiting for transfers between devices: 186 us -> none  [the longest x2 88.4 us: shards(): lax.all_gather(hidden, 'gx', axis=1, tiled=True)]
    dot_general x6 -> x0, matrix products: 97.3 us -> none  [the longest x2 38 us: shards(): gate_next = jnp.dot(piece, gate_weight, preferred_element_type=jnp.float32)]
    reduce_scatter x2 -> x0, waiting for transfers between devices: 50.1 us -> none  [shards(): lax.psum_scatter(partial_value, 'gy', scatter_dimension=0, tiled=True)]
  transfers between devices with their start and end apart: 8 -> 0, of which waited for: 8 -> 0; matrix products, arithmetic and copies ran while one was open for 28% -> 0% of each run, Pallas kernels for 0% -> 0%
where the time goes in v2:
time: 210 us
  Pallas kernels  208 us (99%)
    pallas_call x1, Pallas kernels, fused(): pl.pallas_call(functools.partial(kernel, nz), out_shape=jax.ShapeDtypeStr...  208 us

profile of v2, /device:TPU:0, one launch (start us, length us, event | category | flops | bytes accessed | tf_op | source)
XLA Modules:
  0.0 210.3 jit_solution(9019114068787791651)
XLA Ops:
  0.0 208.4 %shard_map.46 = bf16[128,2048]{1,0:T(8,128)(2,1)} custom-call(bf16[128,2048]{1,0:T(8,128)(2,1)} %tokens.1, bf16[8192,1664]{1,0:T(8,128)(2,1)} %gate.1, bf16[8192,1664]{1,0:T(8,128)(2,1)} %up.1, bf16[6656,2048]{1,0:T(8,128)(2,1)} %down.1), custom_call_target="tpu_custom_call" | custom-call | flops 41875931136 | bytes 245366784 | tf_op jit(solution)/shard_map/pallas_call | solution.py:350
  208.4 1.9 copy.6

commit v3 on v2

--- a/solution.py
+++ b/solution.py
@@ -8,7 +8,7 @@
 from jax.sharding import PartitionSpec as P
 
 CHUNKS = 2
-PARTS = 4
+PARTS = 2
 TILE = 128
 WIDE = 256
 
@@ -105,9 +105,12 @@
                     then(c, b)
 
     token_view = lambda c, b: token_block(c, g, b)
-    hidden_view = lambda c, b: hid.at[c, b]
+    cut = (tiles + 1) // 2
+    spans = ((0, cut * TILE), (cut * TILE, units - cut * TILE))
+    pieces_z = [
+        (lambda p, b, span=span: hid.at[p // 2, b, :, pl.ds(*span)], hz_s, hz_r) for span in spans
+    ]
     tokens_z = (token_view, tz_s, tz_r)
-    hidden_z = (hidden_view, hz_s, hz_r)
 
     def to_sib(c, b, who, s, r):
         return remote(token_block(c, who, b), token_block(c, who, b), s.at[c, b], r.at[c, b], gy=sib)
@@ -194,10 +197,16 @@
     tokens_across(0)
 
     last = nz - 1
-    early = 2 * (PARTS - 1) - 1
+    events = nz * (PARTS - 1)
+    stride = (tiles - 1) // events
 
     def hidden_step(n):
-        hop_recv(*hidden_z, n // last, n % last + 1, None)
+        p = n // last
+        for side in range(2):
+
+            @pl.when(p % 2 == side)
+            def _():
+                hop_recv(*pieces_z[side], p, n % last + 1, None)
 
     @pl.loop(0, PARTS)
     def _(c):
@@ -226,9 +235,10 @@
                 a / (1.0 + jnp.exp(-a)) * u
             ).astype(hid.dtype)
 
-            @pl.when((c == 0) & (t < nz * (PARTS - 1)))
-            def _():
-                which, s = 1 + t // nz, t % nz + 1
+            @pl.when((c == 0) & (t % stride == 0) & (t >= stride) & (t <= stride * events))
+            def _():
+                q = t // stride - 1
+                which, s = 1 + q // nz, q % nz + 1
 
                 @pl.when((s == 1) & (which + 1 < PARTS))
                 def _():
@@ -242,15 +252,20 @@
                 def _():
                     tokens_across(which)
 
-            @pl.when((c >= 2) & (t == tiles // 2))
-            def _():
-                hidden_step(2 * (c - 1) - 1)
-
-        hop_start(*hidden_z, c, 1)
-
-        @pl.when(c >= 1)
-        def _():
-            hidden_step(2 * (c - 1))
+            for side, (done, middle) in enumerate(((cut - 1, cut // 2), (tiles - 1, cut + 2))):
+                p = 2 * c + side
+
+                @pl.when((t == middle) & (p >= 2))
+                def _():
+                    hidden_step(2 * (p - 1) - 1)
+
+                @pl.when(t == done)
+                def _():
+                    hop_start(*pieces_z[side], p, 1)
+
+                    @pl.when(p >= 1)
+                    def _():
+                        hidden_step(2 * (p - 1))
 
     load_down.wait()
 
@@ -290,13 +305,21 @@
     def _(d):
         mix(d, z, True)
 
+        @pl.when(d >= 1)
+        def _():
+            hidden_step(7)
+
         @pl.loop(1, nz)
         def _(s):
-            n = d * last + s - 1
-
-            @pl.when(n >= early)
-            def _():
-                hidden_step(n)
+            m = d * nz + s
+
+            @pl.when((m >= 2) & (m <= 5))
+            def _():
+                hidden_step(m + 3)
+
+            @pl.when(m >= 5)
+            def _():
+                hidden_step(m + 4)
 
             @pl.when(z - s >= 0)
             def _():
@@ -325,7 +348,8 @@
         @pl.loop(1, nz)
         def _(s):
             hop_sent(*tokens_z, c, s)
-            hop_sent(*hidden_z, c, s)
+            for side in range(2):
+                hop_sent(*pieces_z[side], 2 * c + side, s)
 
         @pl.loop(0, nz)
         def _(b):
@@ -346,7 +370,7 @@
     bf16 = jnp.bfloat16
     anywhere = pl.BlockSpec(memory_space=pl.ANY)
     hops, each = dma((2, PARTS, nz - 1)), dma((PARTS, nz))
-    one = dma((PARTS,))
+    one, pieces = dma((PARTS,)), dma((2, 2 * PARTS, nz - 1))
     return pl.pallas_call(
         functools.partial(kernel, nz),
         out_shape=jax.ShapeDtypeStruct((own, cols), bf16),
@@ -361,7 +385,7 @@
             pltpu.VMEM((PARTS, 2 * rows, cols), jnp.float32),
             pltpu.VMEM((PARTS, rows, cols), jnp.float32),
             one, dma((2, 2)), dma(()),
-            hops, hops, each, each, each, each, each, each, hops, hops,
+            hops, hops, each, each, each, each, each, each, pieces, pieces,
             one, one, one, one,
         ],
         compiler_params=pltpu.CompilerParams(
@@ -385,9 +409,9 @@
         )
         tiles = units // TILE
         return (
-            mesh.shape["gy"] == 4 and nz > 1 and own % (16 * PARTS) == 0 and units % TILE == 0
+            mesh.shape["gy"] == 4 and nz == 4 and own % (16 * PARTS) == 0 and units % TILE == 0
             and depth % TILE == 0 and cols % WIDE == 0 and held <= 61 * 2**20
-            and tiles >= nz * (PARTS - 1) and (PARTS - 1) * 2 - 1 <= PARTS * (nz - 1)
+            and tiles > nz * (PARTS - 1) and tiles >= 9
         )
     return body
 

time: 210 us -> 200 us (0.952)
  Pallas kernels: 208 us -> 198 us
    pallas_call x1, Pallas kernels: 208 us -> 198 us  [fused(): pl.pallas_call(functools.partial(kernel, nz), out_shape=jax.ShapeDtypeStr...]
where the time goes in v3:
time: 200 us
  Pallas kernels  198 us (99%)
    pallas_call x1, Pallas kernels, fused(): pl.pallas_call(functools.partial(kernel, nz), out_shape=jax.ShapeDtypeStr...  198 us

profile of v3, /device:TPU:0, one launch (start us, length us, event | category | flops | bytes accessed | tf_op | source)
XLA Modules:
  0.0 199.9 jit_solution(3973918980587208827)
XLA Ops:
  0.0 198.0 %shard_map.46 = bf16[128,2048]{1,0:T(8,128)(2,1)} custom-call(bf16[128,2048]{1,0:T(8,128)(2,1)} %tokens.1, bf16[8192,1664]{1,0:T(8,128)(2,1)} %gate.1, bf16[8192,1664]{1,0:T(8,128)(2,1)} %up.1, bf16[6656,2048]{1,0:T(8,128)(2,1)} %down.1), custom_call_target="tpu_custom_call" | custom-call | flops 41875931136 | bytes 136314880 | tf_op jit(solution)/shard_map/pallas_call | solution.py:374
  198.0 1.9 copy.6
